TPU v7x, 32 devices: a whole 2x2x4 slice. The times are simulated.
32 devices in a mesh: seq: 8 (over z, x), ch: 4 (over y, core).
Axes of the slice: x: 2, y: 2, z: 4, core: 2. Of those that a mesh axis runs over, the one named last changes fastest.
Arguments:
- block_input: bfloat16 [8192, 2048], P('ch', 'seq'), may hold values from -110 to 110
- norm_gain: float32 [8192], P('ch'), may hold values from 0.1 to 1.9
- short_taps: bfloat16 [8192, 7], P('ch'), may hold values from -2 to 2
- medium_taps: bfloat16 [8192, 128], P('ch'), may hold values from -0.5 to 0.5
- long_filter: float32 [8192, 2048], P(('ch', 'seq')), may hold values from -2 to 2
- grad_out: bfloat16 [8192, 2048], P('ch', 'seq'), may hold values from -2.390625 to 2.390625
Outputs:
- grad_normed: bfloat16 [8192, 2048], P('ch', 'seq')
- grad_long: float32 [8192, 2048], P(('ch', 'seq'))
- grad_medium: float32 [8192, 128], P(('ch', 'seq'))
- grad_short: float32 [8192, 7], P(('ch', 'seq'))
All inputs are finite; a program needn't handle non-finite values.
Results may differ from a plain program's by a relative error of at most 0.0058.
Values may be sent and summed in bfloat16 or wider, within the bound.
A program may use at most 128 MiB of HBM per device.

v0:
```python
import math
import jax
import jax.numpy as jnp
from jax import lax
from jax.sharding import PartitionSpec as P

highest = lax.Precision.HIGHEST


def depthwise(signal, taps):
    result = lax.conv_general_dilated(
        signal[None],
        taps[:, None, :],
        (1,),
        "VALID",
        dimension_numbers=("NCH", "OIH", "NCH"),
        feature_group_count=signal.shape[0],
        preferred_element_type=jnp.float32,
    )
    return result[0]


def fourier_tables(length):
    total = 2 * length
    inner = 128
    outer = total // inner
    half = outer // 2
    two_pi = 2.0 * math.pi
    freq_outer = jnp.arange(outer, dtype=jnp.int32)
    pos_half = jnp.arange(half, dtype=jnp.int32)
    pos_inner = jnp.arange(inner, dtype=jnp.int32)
    outer_angle = (
        two_pi * (freq_outer[:, None] * pos_half[None, :] % outer).astype(jnp.float32) / outer
    )
    inner_angle = (
        two_pi * (pos_inner[:, None] * pos_inner[None, :] % inner).astype(jnp.float32) / inner
    )
    twist_angle = (
        two_pi * (freq_outer[:, None] * pos_inner[None, :] % total).astype(jnp.float32) / total
    )
    return (
        jnp.cos(outer_angle),
        jnp.sin(outer_angle),
        jnp.cos(inner_angle),
        jnp.sin(inner_angle),
        jnp.cos(twist_angle),
        jnp.sin(twist_angle),
    )


def forward_dft(signal, tables):
    cos_outer, sin_outer, cos_inner, sin_inner, cos_twist, sin_twist = tables
    blocks = signal.reshape(signal.shape[0], cos_outer.shape[1], cos_inner.shape[0])
    real = jnp.einsum("kn,cnq->ckq", cos_outer, blocks, precision=highest)
    imag = -jnp.einsum("kn,cnq->ckq", sin_outer, blocks, precision=highest)
    turned_re = real * cos_twist + imag * sin_twist
    turned_im = imag * cos_twist - real * sin_twist
    out_re = jnp.einsum("ckq,qr->ckr", turned_re, cos_inner, precision=highest) + jnp.einsum(
        "ckq,qr->ckr", turned_im, sin_inner, precision=highest
    )
    out_im = jnp.einsum("ckq,qr->ckr", turned_im, cos_inner, precision=highest) - jnp.einsum(
        "ckq,qr->ckr", turned_re, sin_inner, precision=highest
    )
    return (out_re, out_im)


def inverse_dft(spec_re, spec_im, tables):
    cos_outer, sin_outer, cos_inner, sin_inner, cos_twist, sin_twist = tables
    total = cos_outer.shape[0] * cos_inner.shape[0]
    step_re = jnp.einsum("ckq,qr->ckr", spec_re, cos_inner, precision=highest) - jnp.einsum(
        "ckq,qr->ckr", spec_im, sin_inner, precision=highest
    )
    step_im = jnp.einsum("ckq,qr->ckr", spec_im, cos_inner, precision=highest) + jnp.einsum(
        "ckq,qr->ckr", spec_re, sin_inner, precision=highest
    )
    turned_re = step_re * cos_twist - step_im * sin_twist
    turned_im = step_im * cos_twist + step_re * sin_twist
    blocks = jnp.einsum("kn,ckq->cnq", cos_outer, turned_re, precision=highest) - jnp.einsum(
        "kn,ckq->cnq", sin_outer, turned_im, precision=highest
    )
    return (blocks / total).reshape(spec_re.shape[0], -1)


def on_device(block_input, norm_gain, short_taps, medium_taps, long_filter, grad_out):
    chans, tokens = block_input.shape
    seq_count = lax.axis_size("seq")
    med_count = medium_taps.shape[1]
    reach = med_count + short_taps.shape[1] - 2
    inputs32 = block_input.astype(jnp.float32)
    squares = lax.psum(jnp.sum(inputs32 * inputs32, axis=0), "ch")
    inv_rms = lax.rsqrt(squares / (chans * lax.axis_size("ch")) + 1e-05)
    normed = (inputs32 * inv_rms[None, :] * norm_gain[:, None]).astype(jnp.bfloat16)
    arrived, grad_chan = (
        lax.all_to_all(normed, "seq", split_axis=0, concat_axis=1, tiled=True),
        lax.all_to_all(grad_out, "seq", split_axis=0, concat_axis=1, tiled=True),
    )
    group, length = arrived.shape
    scale = length ** (-0.5)
    offset = lax.axis_index("seq") * group
    short_local = lax.dynamic_slice_in_dim(short_taps, offset, group, 0)
    medium_local = lax.dynamic_slice_in_dim(medium_taps, offset, group, 0)
    normed_pad = jnp.pad(arrived, ((0, 0), (reach, 0)))
    shorted_pad = depthwise(normed_pad, short_local[:, ::-1]).astype(jnp.bfloat16)
    filtered_chan = depthwise(shorted_pad, medium_local[:, ::-1]).astype(jnp.bfloat16)
    tables = fourier_tables(length)
    grad_re, grad_im = forward_dft(grad_chan.astype(jnp.float32), tables)
    filt_re, filt_im = forward_dft(long_filter, tables)
    sig_re, sig_im = forward_dft(filtered_chan.astype(jnp.float32), tables)
    grad_filtered = inverse_dft(
        filt_re * grad_re + filt_im * grad_im, filt_re * grad_im - filt_im * grad_re, tables
    ).astype(jnp.bfloat16)
    grad_long = (
        inverse_dft(
            sig_re * grad_re + sig_im * grad_im, sig_re * grad_im - sig_im * grad_re, tables
        )
        * scale
    )
    back_pad = jnp.pad(grad_filtered, ((0, 0), (0, reach)))
    shorted_grad = depthwise(back_pad, medium_local).astype(jnp.bfloat16)
    normed_grad = depthwise(shorted_grad, short_local).astype(jnp.bfloat16)
    medium_local_grad = depthwise(shorted_pad, grad_filtered)[:, ::-1] * scale
    short_local_grad = (
        depthwise(normed_pad[:, med_count - 1 :], shorted_grad[:, :length])[:, ::-1] * scale
    )
    leaving = normed_grad.reshape(group, seq_count, tokens)
    returned = lax.all_to_all(leaving, "seq", split_axis=1, concat_axis=0, tiled=True).reshape(
        chans, -1
    )
    return (returned, grad_long, medium_local_grad, short_local_grad)


def solution(mesh):
    placed = (
        P("ch", "seq"),
        P("ch"),
        P("ch", None),
        P("ch", None),
        P(("ch", "seq"), None),
        P("ch", "seq"),
    )
    return jax.shard_map(
        on_device,
        mesh=mesh,
        in_specs=placed,
        out_specs=(
            P("ch", "seq"),
            P(("ch", "seq"), None),
            P(("ch", "seq"), None),
            P(("ch", "seq"), None),
        ),
        check_vma=False,
    )
```

profile of v0, /device:TPU:0, one launch (start us, length us, event | category | flops | bytes accessed | tf_op | source)
XLA Modules:
  0.0 433.6 jit_solution(14907793232586408200)
XLA Ops:
  2.2 8.4 %psum.7 = f32[256]{0:T(256)S(1)} all-reduce(f32[256]{0:T(256)S(1)} %fusion.44), channel_id=1, replica_groups=mesh['seq'=8,'ch'=4] {'ch'}, use_global_device_ids=true, to_apply=%region_1.0 | all-reduce | flops 256 | bytes 2048 | tf_op jit(solution)/shard_map/psum | solution.py:90
  13.5 5.8 %all-to-all-start.2 = ((bf16[8,256,256]{1,2,0:T(8,128)(2,1)}), bf16[8,256,256]{1,2,0:T(8,128)(2,1)}, u32[]{:S(2)}, u32[]{:S(2)}) async-start(bf16[8,256,256]{1,2,0:T(8,128)(2,1)} %copy.122), calls=%async_computation.2 | async-start | bytes 2097152 | tf_op jit(solution)/shard_map/all_to_all | solution.py:94
  24.6 5.1 %fusion.171 = f32[32,256,128]{2,0,1:T(8,128)} fusion(f32[256,16,128]{2,1,0:T(8,128)S(1)} %bitcast.202), kind=kOutput, calls=%fused_computation.179 | convolution fusion | flops 201333760 | bytes 6291456 | tf_op jit(solution)/shard_map/kn,cnq->ckq/dot_general | solution.py:54
  29.7 5.1 %fusion.163 = f32[32,256,128]{2,0,1:T(8,128)} fusion(f32[256,16,128]{2,1,0:T(8,128)S(1)} %bitcast.203), kind=kOutput, calls=%fused_computation.171 | convolution fusion | flops 201333760 | bytes 6291456 | tf_op jit(solution)/shard_map/kn,cnq->ckq/dot_general | solution.py:55
  34.9 9.3 %all-to-all-done.2 = bf16[8,256,256]{1,2,0:T(8,128)(2,1)} async-done(((bf16[8,256,256]{1,2,0:T(8,128)(2,1)}), bf16[8,256,256]{1,2,0:T(8,128)(2,1)}, u32[]{:S(2)}, u32[]{:S(2)}) %all-to-all-start.2) | async-done | bytes 1048608 | tf_op jit(solution)/shard_map/all_to_all | solution.py:94
  54.4 24.1 %fusion.66 = bf16[8,273,256]{2,0,1:T(8,128)(2,1)S(1)} fusion(bf16[256,1,128]{0,1,2:T(2,128)(2,1)S(1)} %copy.126, bf16[1,7,127,256]{3,1,2,0:T(8,128)(2,1)S(1)} %slice.20, bf16[1,8,273,256]{3,1,2,0:T(8,128)(2,1)S(1)} %select_bitcast_fusion), kind=kOutput, calls=%fused_computation.86 | convolution fusion | flops 148604928 | bytes 2757120 | tf_op jit(solution)/shard_map/conv_general_dilated | solution.py:11
  96.1 6.0 %add_bitcast_fusion = (f32[256,32,128]{2,1,0:T(8,128)S(1)}, f32[256,32,128]{2,1,0:T(8,128)S(1)}, f32[256,32,128]{2,1,0:T(8,128)S(1)}, f32[256,32,128]{2,1,0:T(8,128)S(1)}) fusion(f32[32,256,128]{2,0,1:T(8,128)S(1)} %fusion.161, f32[32,128]{1,0:T(8,128)S(1)} %get-tuple-element.38, f32[32,128]{1,0:T(8,128)S(1)} %get-tuple-element.39, ...), kind=kOutput, calls=%fused_computation.24 | convolution fusion | flops 216013824 | bytes 30441472 | tf_op jit(solution)/shard_map/kn,cnq->ckq/dot_general | solution.py:54
  102.1 8.6 %fusion.12 = f32[256,32,128]{2,0,1:T(8,128)} fusion(f32[256,32,128]{2,1,0:T(8,128)S(1)} %get-tuple-element.29), kind=kOutput, calls=%fused_computation.29 | convolution fusion | flops 1610842112 | bytes 8388608 | tf_op jit(solution)/shard_map/ckq,qr->ckr/dot_general | solution.py:58
  110.7 6.8 %fusion.10 = f32[256,32,128]{2,0,1:T(8,128)S(1)} fusion(f32[256,32,128]{2,1,0:T(8,128)S(1)} %get-tuple-element.29), kind=kOutput, calls=%fused_computation.27 | convolution fusion | flops 1610842112 | bytes 8388608 | tf_op jit(solution)/shard_map/ckq,qr->ckr/dot_general | solution.py:61
  117.5 7.2 %fusion.18 = f32[256,32,128]{2,0,1:T(8,128)S(1)} fusion(f32[256,32,128]{2,1,0:T(8,128)S(1)} %get-tuple-element.36), kind=kOutput, calls=%fused_computation.35 | convolution fusion | flops 1610842112 | bytes 8388608 | tf_op jit(solution)/shard_map/ckq,qr->ckr/dot_general | solution.py:61
  124.7 7.1 %fusion.20 = f32[256,32,128]{2,0,1:T(8,128)S(1)} fusion(f32[256,32,128]{2,1,0:T(8,128)S(1)} %get-tuple-element.36), kind=kOutput, calls=%fused_computation.37 | convolution fusion | flops 1610842112 | bytes 8388608 | tf_op jit(solution)/shard_map/ckq,qr->ckr/dot_general | solution.py:58
  131.8 13.2 %fusion.92 = f32[256,32,128]{2,0,1:T(8,128)} fusion(f32[256,128,32]{1,2,0:T(8,128)S(1)} %copy-done.2, f32[256,128,32]{1,2,0:T(8,128)S(1)} %copy-done.3, f32[32,128]{1,0:T(8,128)S(1)} %get-tuple-element.38, f32[32,128]{1,0:T(8,128)S(1)} %get-tuple-element.39), kind=kOutput, calls=%fused_computation.109 | convolution fusion | flops 1615036416 | bytes 12615680 | tf_op jit(solution)/shard_map/ckq,qr->ckr/dot_general | solution.py:58
  145.0 12.9 %fusion.88 = f32[256,32,128]{2,0,1:T(8,128)} fusion(f32[256,128,32]{1,2,0:T(8,128)S(1)} %copy-done.2, f32[256,128,32]{1,2,0:T(8,128)S(1)} %copy-done.3, f32[32,128]{1,0:T(8,128)S(1)} %get-tuple-element.38, f32[32,128]{1,0:T(8,128)S(1)} %get-tuple-element.39), kind=kOutput, calls=%fused_computation.108 | convolution fusion | flops 1615036416 | bytes 12615680 | tf_op jit(solution)/shard_map/ckq,qr->ckr/dot_general | solution.py:61
  159.2 14.5 %convolution_add_fusion.1 = f32[256,32,128]{2,0,1:T(8,128)} fusion(f32[256,32,128]{2,0,1:T(8,128)} %fusion.92, f32[256,128,32]{1,2,0:T(8,128)S(1)} %copy-done.2, f32[256,128,32]{1,2,0:T(8,128)S(1)} %copy-done.3, f32[32,128]{1,0:T(8,128)S(1)} %get-tuple-element.38, f32[32,128]{1,0:T(8,128)S(1)} %get-tuple-element.39), kind=kOutput, calls=%fused_computation.62 | convolution fusion | flops 1616084992 | bytes 16809984 | tf_op jit(solution)/shard_map/ckq,qr->ckr/dot_general | solution.py:58
  173.7 8.4 %fusion.36 = f32[256,32,128]{2,0,1:T(8,128)} fusion(f32[256,32,128]{2,0,1:T(8,128)S(1)} %copy-done.8, f32[256,32,128]{2,1,0:T(8,128)S(1)} %get-tuple-element.28), kind=kOutput, calls=%fused_computation.57 | convolution fusion | flops 1611890688 | bytes 12582912 | tf_op jit(solution)/shard_map/ckq,qr->ckr/dot_general | solution.py:58
  182.1 8.6 %fusion.39 = f32[256,32,128]{2,0,1:T(8,128)} fusion(f32[256,32,128]{2,0,1:T(8,128)S(1)} %fusion.10, f32[256,32,128]{2,1,0:T(8,128)S(1)} %get-tuple-element.28), kind=kOutput, calls=%fused_computation.58 | convolution fusion | flops 1611890688 | bytes 12582912 | tf_op jit(solution)/shard_map/ckq,qr->ckr/dot_general | solution.py:61
  190.7 8.6 %fusion.33 = f32[256,32,128]{2,0,1:T(8,128)} fusion(f32[256,32,128]{2,0,1:T(8,128)S(1)} %fusion.18, f32[256,32,128]{2,1,0:T(8,128)S(1)} %get-tuple-element.37), kind=kOutput, calls=%fused_computation.56 | convolution fusion | flops 1611890688 | bytes 12582912 | tf_op jit(solution)/shard_map/ckq,qr->ckr/dot_general | solution.py:61
  199.3 8.4 %fusion.30 = f32[256,32,128]{2,0,1:T(8,128)} fusion(f32[256,32,128]{2,0,1:T(8,128)S(1)} %fusion.20, f32[256,32,128]{2,1,0:T(8,128)S(1)} %get-tuple-element.37), kind=kOutput, calls=%fused_computation.55 | convolution fusion | flops 1611890688 | bytes 12582912 | tf_op jit(solution)/shard_map/ckq,qr->ckr/dot_general | solution.py:58
  207.7 22.7 %multiply_subtract_fusion.1 = (f32[256,32,128]{2,0,1:T(8,128)}, f32[256,32,128]{2,0,1:T(8,128)}, f32[256,32,128]{2,0,1:T(8,128)}, f32[256,32,128]{2,0,1:T(8,128)}) fusion(f32[256,32,128]{2,0,1:T(8,128)} %fusion.36, f32[256,32,128]{2,0,1:T(8,128)} %convolution_add_fusion.1, f32[256,32,128]{2,0,1:T(8,128)} %fusion.39, f32[256,32,128]{2,0,1:T(8,128)} %fusion.33, ...), kind=kOutput, calls=%fused_computation.17 | convolution fusion | flops 1628667904 | bytes 50364416 | tf_op jit(solution)/shard_map/ckq,qr->ckr/dot_general | solution.py:61
  230.4 6.0 %fusion.111 = f32[256,32,128]{2,0,1:T(8,128)S(1)} fusion(f32[256,32,128]{2,0,1:T(8,128)} %get-tuple-element.21), kind=kOutput, calls=%fused_computation.131 | convolution fusion | flops 1610842112 | bytes 8388608 | tf_op jit(solution)/shard_map/ckq,qr->ckr/dot_general | solution.py:70
  236.5 5.6 %fusion.109 = f32[256,32,128]{2,0,1:T(8,128)} fusion(f32[256,32,128]{2,0,1:T(8,128)S(1)} %copy-done.6), kind=kOutput, calls=%fused_computation.129 | convolution fusion | flops 1610842112 | bytes 8388608 | tf_op jit(solution)/shard_map/ckq,qr->ckr/dot_general | solution.py:73
  257.7 5.5 %convolution_add_fusion.2 = f32[256,32,128]{2,0,1:T(8,128)} fusion(f32[256,32,128]{2,0,1:T(8,128)S(1)} %fusion.115, f32[256,32,128]{2,0,1:T(8,128)S(1)} %copy-done.4), kind=kOutput, calls=%fused_computation.63 | convolution fusion | flops 1611890688 | bytes 12582912 | tf_op jit(solution)/shard_map/ckq,qr->ckr/dot_general | solution.py:73
  263.3 11.6 %multiply_subtract_fusion = (f32[256,32,128]{2,0,1:T(8,128)}, f32[256,32,128]{2,0,1:T(8,128)}, f32[256,32,128]{2,0,1:T(8,128)}, f32[256,32,128]{2,0,1:T(8,128)}) fusion(f32[256,32,128]{2,0,1:T(8,128)S(1)} %convolution_subtract_fusion, f32[32,128]{1,0:T(8,128)S(1)} %get-tuple-element.38, f32[32,128]{1,0:T(8,128)S(1)} %get-tuple-element.39, ...), kind=kOutput, calls=%fused_computation.16 | convolution fusion | flops 1624473600 | bytes 37781504 | tf_op jit(solution)/shard_map/ckq,qr->ckr/dot_general | solution.py:73
  274.9 7.0 %fusion.6 = f32[256,128,16]{1,2,0:T(8,128)S(1)} fusion(f32[256,32,128]{2,0,1:T(8,128)} %get-tuple-element.34), kind=kOutput, calls=%fused_computation.11 | convolution fusion | flops 201333760 | bytes 6291456 | tf_op jit(solution)/shard_map/kn,ckq->cnq/dot_general | solution.py:78
  289.9 28.6 %select_convert_fusion.1 = bf16[8,273,256]{2,0,1:T(8,128)(2,1)S(1)} fusion(bf16[256,1,128]{0,1,2:T(2,128)(2,1)S(1)} %copy-done.14, bf16[256,1,7,127]{0,2,3,1:T(8,128)(2,1)S(1)} %slice.16, bf16[256,1,8,273]{0,2,3,1:T(8,128)(2,1)S(1)} %copy.117, pred[8,273]{0,1:T(8,128)(4,1)S(1)} %copy-done.15), kind=kOutput, calls=%fused_computation.54 | convolution fusion | flops 149164032 | bytes 2759304 | tf_op jit(solution)/shard_map/conv_general_dilated | solution.py:11
  324.7 5.9 %all-to-all-start.1 = ((bf16[256,8,256]{0,2,1:T(8,128)(2,1)}), bf16[256,8,256]{0,2,1:T(8,128)(2,1)}, u32[]{:S(2)}, u32[]{:S(2)}) async-start(bf16[256,8,256]{0,2,1:T(8,128)(2,1)} %bitcast.19), calls=%async_computation.1 | async-start | bytes 2097152 | tf_op jit(solution)/shard_map/all_to_all | solution.py:126
  330.6 6.8 %fusion.2 = f32[256,128,16]{1,2,0:T(8,128)S(1)} fusion(f32[256,32,128]{2,0,1:T(8,128)} %get-tuple-element.25), kind=kOutput, calls=%fused_computation.6 | convolution fusion | flops 201333760 | bytes 6291456 | tf_op jit(solution)/shard_map/kn,ckq->cnq/dot_general | solution.py:78
  337.5 6.5 %reshape.129 = bf16[1,2184,256]{2,0,1:T(2,128)(2,1)} reshape(bf16[8,273,256]{2,1,0:T(8,128)(2,1)} %copy.133) | data formatting | bytes 2236416 | tf_op jit(solution)/shard_map/convert_element_type | solution.py:103
  343.9 5.9 %copy.135 = bf16[256,1,2048]{0,1,2:T(2,128)(2,1)} copy(bf16[256,1,2048]{2,0,1:T(8,128)(2,1)} %convert_element_type.181) | data formatting | bytes 2097152 | tf_op jit(solution)/shard_map/convert_element_type | solution.py:111
  349.9 25.4 %fusion.326 = f32[1,256,128]{1,0,2:T(1,128)S(1)} fusion(bf16[1,2184,256]{2,0,1:T(2,128)(2,1)} %reshape.129, bf16[256,1,2048]{0,1,2:T(2,128)(2,1)} %copy.135), kind=kOutput, calls=%fused_computation.326 | convolution fusion | flops 134217728 | bytes 2297856 | tf_op jit(solution)/shard_map/conv_general_dilated | solution.py:11
  380.3 6.9 %subtract_multiply_fusion = f32[256,128,16]{1,2,0:T(8,128)S(1)} fusion(f32[256,128,16]{1,2,0:T(8,128)S(1)} %fusion.2, f32[256,32,128]{2,0,1:T(8,128)} %get-tuple-element.24), kind=kOutput, calls=%fused_computation.72 | convolution fusion | flops 202382336 | bytes 8388608 | tf_op jit(solution)/shard_map/kn,ckq->cnq/dot_general | solution.py:78
  391.8 38.4 %fusion.42 = f32[1,256,7]{1,0,2:T(1,128)S(1)} fusion(bf16[1,256,2054]{1,2,0:T(8,128)(2,1)S(1)} %slice_bitcast_fusion.1, bf16[256,1,2048]{0,2,1:T(8,128)(2,1)S(1)} %slice_bitcast_fusion.2), kind=kOutput, calls=%fused_computation.65 | convolution fusion | flops 7340032 | bytes 2107392 | tf_op jit(solution)/shard_map/conv_general_dilated | solution.py:11
  (103 shorter events, 80.8 us)
Async XLA Ops:
  0.6 18.7 %copy-start = (bf16[2048,128]{1,0:T(8,128)(2,1)S(1)}, bf16[2048,128]{1,0:T(8,128)(2,1)}, u32[]{:S(2)}) copy-start(bf16[2048,128]{1,0:T(8,128)(2,1)} %param.9) | copy-start | bytes 1572868
  13.5 30.7 %all-to-all-start.2 = ((bf16[8,256,256]{1,2,0:T(8,128)(2,1)}), bf16[8,256,256]{1,2,0:T(8,128)(2,1)}, u32[]{:S(2)}, u32[]{:S(2)}) async-start(bf16[8,256,256]{1,2,0:T(8,128)(2,1)} %copy.122), calls=%async_computation.2 | async-start | bytes 2097152 | tf_op jit(solution)/shard_map/all_to_all | solution.py:94
  44.2 45.7 %all-to-all-start = ((bf16[8,256,256]{2,1,0:T(8,128)(2,1)}), bf16[8,256,256]{2,1,0:T(8,128)(2,1)}, u32[]{:S(2)}, u32[]{:S(2)}) async-start(bf16[8,256,256]{2,1,0:T(8,128)(2,1)} %bitcast.210), calls=%async_computation | async-start | bytes 2097152 | tf_op jit(solution)/shard_map/all_to_all | solution.py:95
  48.4 2.2 copy-start.16
  53.4 25.2 %copy-start.11 = (bf16[8,273,256]{2,0,1:T(8,128)(2,1)}, bf16[8,273,256]{2,0,1:T(8,128)(2,1)S(1)}, u32[]{:S(2)}) copy-start(bf16[8,273,256]{2,0,1:T(8,128)(2,1)S(1)} %select_convert_fusion) | copy-start | bytes 3354628
  92.8 3.3 copy-start.9
  124.7 7.1 %copy-start.2 = (f32[256,128,32]{1,2,0:T(8,128)S(1)}, f32[256,128,32]{1,2,0:T(8,128)}, u32[]{:S(2)}) copy-start(f32[256,128,32]{1,2,0:T(8,128)} %fusion.166) | copy-start | bytes 12582916
  124.7 7.1 %copy-start.3 = (f32[256,128,32]{1,2,0:T(8,128)S(1)}, f32[256,128,32]{1,2,0:T(8,128)}, u32[]{:S(2)}) copy-start(f32[256,128,32]{1,2,0:T(8,128)} %fusion.158) | copy-start | bytes 12582916
  145.0 12.9 %copy-start.12 = (bf16[8,273,256]{2,0,1:T(8,128)(2,1)S(1)}, bf16[8,273,256]{2,0,1:T(8,128)(2,1)}, u32[]{:S(2)}) copy-start(bf16[8,273,256]{2,0,1:T(8,128)(2,1)} %copy-done.11) | copy-start | bytes 3354628
  159.2 14.5 %copy-start.8 = (f32[256,32,128]{2,0,1:T(8,128)S(1)}, f32[256,32,128]{2,0,1:T(8,128)}, u32[]{:S(2)}) copy-start(f32[256,32,128]{2,0,1:T(8,128)} %fusion.12) | copy-start | bytes 12582916
  230.4 6.0 %copy-start.6 = (f32[256,32,128]{2,0,1:T(8,128)S(1)}, f32[256,32,128]{2,0,1:T(8,128)}, u32[]{:S(2)}) copy-start(f32[256,32,128]{2,0,1:T(8,128)} %get-tuple-element.20) | copy-start | bytes 12582916
  242.1 3.8 copy-start.4
  245.9 3.8 copy-start.5
  257.7 5.6 %copy-start.7 = (f32[256,32,128]{2,0,1:T(8,128)S(1)}, f32[256,32,128]{2,0,1:T(8,128)}, u32[]{:S(2)}) copy-start(f32[256,32,128]{2,0,1:T(8,128)} %get-tuple-element.21) | copy-start | bytes 12582916
  274.9 7.0 %copy-start.10 = (f32[256,32,128]{2,0,1:T(8,128)S(1)}, f32[256,32,128]{2,0,1:T(8,128)}, u32[]{:S(2)}) copy-start(f32[256,32,128]{2,0,1:T(8,128)} %get-tuple-element.35) | copy-start | bytes 12582916
  289.0 0.9 copy-start.14
  289.0 0.9 copy-start.15
  318.5 2.2 copy-start.17
  324.7 106.2 %all-to-all-start.1 = ((bf16[256,8,256]{0,2,1:T(8,128)(2,1)}), bf16[256,8,256]{0,2,1:T(8,128)(2,1)}, u32[]{:S(2)}, u32[]{:S(2)}) async-start(bf16[256,8,256]{0,2,1:T(8,128)(2,1)} %bitcast.19), calls=%async_computation.1 | async-start | bytes 2097152 | tf_op jit(solution)/shard_map/all_to_all | solution.py:126
  387.2 4.5 %copy-start.13 = (bf16[256,2054]{0,1:T(8,128)(2,1)S(1)}, bf16[256,2054]{0,1:T(8,128)(2,1)}, u32[]{:S(2)}) copy-start(bf16[256,2054]{0,1:T(8,128)(2,1)} %slice_bitcast_fusion) | copy-start | bytes 3154948
  391.8 41.4 %copy-start.1 = (bf16[2048,128]{1,0:T(8,128)(2,1)S(1)}, bf16[2048,128]{1,0:T(8,128)(2,1)}, u32[]{:S(2)}) copy-start(bf16[2048,128]{1,0:T(8,128)(2,1)} %param.9) | copy-start | bytes 1572868
where the time goes:
time: 440 us; the launch traced here: 434 us
  matrix products  346 us (79%)
  local copies, waits for them, and re-layouts  46.6 us (11%)
  starting transfers between devices  15.9 us (4%)
  waiting for transfers between devices  9.3 us (2%)
  blocking collectives  8.36 us (2%)
  other arithmetic  5.68 us (1%)
    conv_general_dilated x6, matrix products, depthwise(): lax.conv_general_dilated(signal[None], taps[:, None, :], (1,), 'VALID', d...  122 us
    dot_general x3, matrix products, forward_dft(): jnp.einsum('ckq,qr->ckr', turned_re, sin_inner, precision=highest)  39.9 us
    dot_general x3, matrix products, forward_dft(): jnp.einsum('ckq,qr->ckr', turned_im, sin_inner, precision=highest)  30.2 us
    dot_general x3, matrix products, forward_dft(): jnp.einsum('ckq,qr->ckr', turned_re, cos_inner, precision=highest)  30 us
    dot_general x3, matrix products, forward_dft(): jnp.einsum('ckq,qr->ckr', turned_im, cos_inner, precision=highest)  26.9 us
    dot_general x2, matrix products, inverse_dft(): jnp.einsum('ckq,qr->ckr', spec_re, sin_inner, precision=highest)  17.2 us
    dot_general x3, matrix products, forward_dft(): real = jnp.einsum('kn,cnq->ckq', cos_outer, blocks, precision=highest)  15 us
    dot_general x2, matrix products, inverse_dft(): jnp.einsum('kn,ckq->cnq', sin_outer, turned_im, precision=highest)  13.8 us
  transfers between devices with their start and end apart: 3, of which 1 were waited for; matrix products, arithmetic and copies ran while one was open for 36% of the time, Pallas kernels for 0%

commit v1 on v0

--- a/solution.py
+++ b/solution.py
@@ -1,3 +1,4 @@
+import functools
 import math
 import jax
 import jax.numpy as jnp
@@ -5,6 +6,31 @@
 from jax.sharding import PartitionSpec as P
 
 highest = lax.Precision.HIGHEST
+
+
+def build_the_shapes(q_in, at_axis, field):
+    even, z_new = (q_in.shape[:at_axis], q_in.shape[at_axis + 1 :])
+    return jnp.moveaxis(q_in.reshape(*even, field, -1, *z_new), at_axis, 0)
+
+
+def post_teams_on(message, array_axis):
+    reached = list(message.shape[1:])
+    reached[array_axis] *= message.shape[0]
+    return jnp.moveaxis(message, 0, array_axis).reshape(reached)
+
+
+def seats_all_bind(incoming_x, along_axis, block_here, shard_in):
+    odd, back = (lax.axis_size(along_axis), lax.axis_index(along_axis))
+    high = build_the_shapes(incoming_x, block_here, odd)
+    stack_in = [high[back]]
+    for dev in range(1, odd):
+        g_now = high[back ^ dev]
+        stack_in.append(lax.ppermute(g_now, along_axis, [(no, no ^ dev) for no in range(odd)]))
+    high = jnp.stack(stack_in, 0)[back ^ jnp.arange(odd)]
+    return post_teams_on(high, shard_in)
+
+
+_match_wall = functools.partial(seats_all_bind, along_axis="seq", block_here=0, shard_in=1)
 
 
 def depthwise(signal, taps):
@@ -91,7 +117,7 @@
     inv_rms = lax.rsqrt(squares / (chans * lax.axis_size("ch")) + 1e-05)
     normed = (inputs32 * inv_rms[None, :] * norm_gain[:, None]).astype(jnp.bfloat16)
     arrived, grad_chan = (
-        lax.all_to_all(normed, "seq", split_axis=0, concat_axis=1, tiled=True),
+        _match_wall(normed),
         lax.all_to_all(grad_out, "seq", split_axis=0, concat_axis=1, tiled=True),
     )
     group, length = arrived.shape

time: 440 us -> 428 us (0.973)
  matrix products: 346 us -> 332 us
  starting transfers between devices: 15.9 us -> 24.2 us
  waiting for transfers between devices: 9.3 us -> 4.17 us
    ppermute x0 -> x7, starting transfers between devices: none -> 11.2 us  [seats_all_bind(): lax.ppermute(g_now, along_axis, [(no, no ^ dev) for no in range(odd)])]
    conv_general_dilated x6, matrix products: 122 us -> 112 us  [depthwise(): lax.conv_general_dilated(signal[None], taps[:, None, :], (1,), 'VALID', d...]
    all_to_all x1 -> x0, waiting for transfers between devices: 9.3 us -> none  [on_device(): lax.all_to_all(normed, 'seq', split_axis=0, concat_axis=1, tiled=True)]
    all_to_all x1 -> x0, starting transfers between devices: 5.81 us -> none  [on_device(): lax.all_to_all(normed, 'seq', split_axis=0, concat_axis=1, tiled=True)]
    convert_element_type x4, local copies, waits for them, and re-layouts: 6.09 us -> 0.64 us  [on_device(): shorted_grad = depthwise(back_pad, medium_local).astype(jnp.bfloat16)]
    unnamed x41 -> x43, local copies, waits for them, and re-layouts: 5.13 us -> 9.11 us
  transfers between devices with their start and end apart: 3 -> 9, of which waited for: 1 -> 2; matrix products, arithmetic and copies ran while one was open for 36% -> 45% of each run, Pallas kernels for 0% -> 0%
where the time goes in v1:
time: 428 us; the launch traced here: 420 us
  matrix products  332 us (78%)
  local copies, waits for them, and re-layouts  45.7 us (11%)
  starting transfers between devices  24.2 us (6%)
  blocking collectives  6.72 us (2%)
  other arithmetic  5.63 us (1%)
    conv_general_dilated x6, matrix products, depthwise(): lax.conv_general_dilated(signal[None], taps[:, None, :], (1,), 'VALID', d...  112 us
    dot_general x3, matrix products, forward_dft(): jnp.einsum('ckq,qr->ckr', turned_re, sin_inner, precision=highest)  39.4 us
    dot_general x3, matrix products, forward_dft(): jnp.einsum('ckq,qr->ckr', turned_re, cos_inner, precision=highest)  31.7 us
    dot_general x3, matrix products, forward_dft(): jnp.einsum('ckq,qr->ckr', turned_im, cos_inner, precision=highest)  27.2 us
    dot_general x3, matrix products, forward_dft(): jnp.einsum('ckq,qr->ckr', turned_im, sin_inner, precision=highest)  26.9 us
    dot_general x2, matrix products, inverse_dft(): jnp.einsum('ckq,qr->ckr', spec_re, sin_inner, precision=highest)  17.2 us
    dot_general x3, matrix products, forward_dft(): real = jnp.einsum('kn,cnq->ckq', cos_outer, blocks, precision=highest)  15 us
    dot_general x2, matrix products, inverse_dft(): jnp.einsum('kn,ckq->cnq', sin_outer, turned_im, precision=highest)  14 us
  transfers between devices with their start and end apart: 9, of which 2 were waited for; matrix products, arithmetic and copies ran while one was open for 45% of the time, Pallas kernels for 0%

profile of v1, /device:TPU:0, one launch (start us, length us, event | category | flops | bytes accessed | tf_op | source)
XLA Modules:
  0.0 420.4 jit_solution(4408019492440649438)
XLA Ops:
  0.6 7.4 %all-to-all-start = ((bf16[8,256,256]{2,1,0:T(8,128)(2,1)}), bf16[8,256,256]{2,1,0:T(8,128)(2,1)}, u32[]{:S(2)}, u32[]{:S(2)}) async-start(bf16[8,256,256]{2,1,0:T(8,128)(2,1)} %bitcast.242), calls=%async_computation | async-start | bytes 2097152 | tf_op jit(solution)/shard_map/all_to_all | solution.py:121
  9.6 6.7 %psum.7 = f32[256]{0:T(256)S(1)} all-reduce(f32[256]{0:T(256)S(1)} %fusion.44), channel_id=1, replica_groups=mesh['seq'=8,'ch'=4] {'ch'}, use_global_device_ids=true, to_apply=%region_1.0 | all-reduce | flops 256 | bytes 2048 | tf_op jit(solution)/shard_map/psum | solution.py:116
  28.2 5.1 %fusion.171 = f32[32,256,128]{2,0,1:T(8,128)} fusion(f32[256,16,128]{2,1,0:T(8,128)S(1)} %bitcast.231), kind=kOutput, calls=%fused_computation.195 | convolution fusion | flops 201333760 | bytes 6291456 | tf_op jit(solution)/shard_map/kn,cnq->ckq/dot_general | solution.py:80
  33.3 5.2 %fusion.163 = f32[32,256,128]{2,0,1:T(8,128)} fusion(f32[256,16,128]{2,1,0:T(8,128)S(1)} %bitcast.232), kind=kOutput, calls=%fused_computation.187 | convolution fusion | flops 201333760 | bytes 6291456 | tf_op jit(solution)/shard_map/kn,cnq->ckq/dot_general | solution.py:81
  62.7 24.1 %fusion.66 = bf16[8,273,256]{2,0,1:T(8,128)(2,1)S(1)} fusion(bf16[256,1,128]{0,1,2:T(2,128)(2,1)S(1)} %copy.124, bf16[1,7,127,256]{3,1,2,0:T(8,128)(2,1)S(1)} %slice.22, bf16[1,8,273,256]{3,1,2,0:T(8,128)(2,1)S(1)} %select_bitcast_fusion), kind=kOutput, calls=%fused_computation.87 | convolution fusion | flops 148604928 | bytes 2757120 | tf_op jit(solution)/shard_map/conv_general_dilated | solution.py:37
  100.4 4.3 %reshape.158 = bf16[1,2184,256]{2,0,1:T(2,128)(2,1)} reshape(bf16[8,273,256]{2,1,0:T(8,128)(2,1)S(1)} %copy.131) | data formatting | bytes 2236416 | tf_op jit(solution)/shard_map/convert_element_type | solution.py:129
  104.8 14.1 %fusion.92 = f32[256,32,128]{2,0,1:T(8,128)S(1)} fusion(f32[256,128,32]{1,2,0:T(8,128)} %fusion.166, f32[256,128,32]{1,2,0:T(8,128)} %fusion.158, f32[32,128]{1,0:T(8,128)S(1)} %get-tuple-element.46, f32[32,128]{1,0:T(8,128)S(1)} %get-tuple-element.47), kind=kOutput, calls=%fused_computation.110 | convolution fusion | flops 1615036416 | bytes 12615680 | tf_op jit(solution)/shard_map/ckq,qr->ckr/dot_general | solution.py:84
  118.9 13.0 %fusion.88 = f32[256,32,128]{2,0,1:T(8,128)} fusion(f32[256,128,32]{1,2,0:T(8,128)S(1)} %copy-done.2, f32[256,128,32]{1,2,0:T(8,128)S(1)} %copy-done.3, f32[32,128]{1,0:T(8,128)S(1)} %get-tuple-element.46, f32[32,128]{1,0:T(8,128)S(1)} %get-tuple-element.47), kind=kOutput, calls=%fused_computation.109 | convolution fusion | flops 1615036416 | bytes 12615680 | tf_op jit(solution)/shard_map/ckq,qr->ckr/dot_general | solution.py:87
  131.9 13.0 %convolution_add_fusion.1 = f32[256,32,128]{2,0,1:T(8,128)} fusion(f32[256,32,128]{2,0,1:T(8,128)S(1)} %fusion.92, f32[256,128,32]{1,2,0:T(8,128)S(1)} %copy-done.2, f32[256,128,32]{1,2,0:T(8,128)S(1)} %copy-done.3, f32[32,128]{1,0:T(8,128)S(1)} %get-tuple-element.46, f32[32,128]{1,0:T(8,128)S(1)} %get-tuple-element.47), kind=kOutput, calls=%fused_computation.63 | convolution fusion | flops 1616084992 | bytes 16809984 | tf_op jit(solution)/shard_map/ckq,qr->ckr/dot_general | solution.py:84
  151.5 6.0 %add_bitcast_fusion = (f32[256,32,128]{2,1,0:T(8,128)S(1)}, f32[256,32,128]{2,1,0:T(8,128)S(1)}, f32[256,32,128]{2,1,0:T(8,128)S(1)}, f32[256,32,128]{2,1,0:T(8,128)S(1)}) fusion(f32[32,256,128]{2,0,1:T(8,128)S(1)} %fusion.161, f32[32,128]{1,0:T(8,128)S(1)} %get-tuple-element.46, f32[32,128]{1,0:T(8,128)S(1)} %get-tuple-element.47, ...), kind=kOutput, calls=%fused_computation.25 | convolution fusion | flops 216013824 | bytes 30441472 | tf_op jit(solution)/shard_map/kn,cnq->ckq/dot_general | solution.py:80
  157.6 7.0 %fusion.12 = f32[256,32,128]{2,0,1:T(8,128)S(1)} fusion(f32[256,32,128]{2,1,0:T(8,128)S(1)} %get-tuple-element.29), kind=kOutput, calls=%fused_computation.30 | convolution fusion | flops 1610842112 | bytes 8388608 | tf_op jit(solution)/shard_map/ckq,qr->ckr/dot_general | solution.py:84
  164.6 7.0 %fusion.10 = f32[256,32,128]{2,0,1:T(8,128)S(1)} fusion(f32[256,32,128]{2,1,0:T(8,128)S(1)} %get-tuple-element.29), kind=kOutput, calls=%fused_computation.28 | convolution fusion | flops 1610842112 | bytes 8388608 | tf_op jit(solution)/shard_map/ckq,qr->ckr/dot_general | solution.py:87
  171.5 7.2 %fusion.18 = f32[256,32,128]{2,0,1:T(8,128)S(1)} fusion(f32[256,32,128]{2,1,0:T(8,128)S(1)} %get-tuple-element.44), kind=kOutput, calls=%fused_computation.36 | convolution fusion | flops 1610842112 | bytes 8388608 | tf_op jit(solution)/shard_map/ckq,qr->ckr/dot_general | solution.py:87
  178.8 7.0 %fusion.20 = f32[256,32,128]{2,0,1:T(8,128)S(1)} fusion(f32[256,32,128]{2,1,0:T(8,128)S(1)} %get-tuple-element.44), kind=kOutput, calls=%fused_computation.38 | convolution fusion | flops 1610842112 | bytes 8388608 | tf_op jit(solution)/shard_map/ckq,qr->ckr/dot_general | solution.py:84
  185.8 8.8 %fusion.36 = f32[256,32,128]{2,0,1:T(8,128)} fusion(f32[256,32,128]{2,0,1:T(8,128)S(1)} %fusion.12, f32[256,32,128]{2,1,0:T(8,128)S(1)} %get-tuple-element.28), kind=kOutput, calls=%fused_computation.58 | convolution fusion | flops 1611890688 | bytes 12582912 | tf_op jit(solution)/shard_map/ckq,qr->ckr/dot_general | solution.py:84
  194.6 8.5 %fusion.39 = f32[256,32,128]{2,0,1:T(8,128)} fusion(f32[256,32,128]{2,0,1:T(8,128)S(1)} %fusion.10, f32[256,32,128]{2,1,0:T(8,128)S(1)} %get-tuple-element.28), kind=kOutput, calls=%fused_computation.59 | convolution fusion | flops 1611890688 | bytes 12582912 | tf_op jit(solution)/shard_map/ckq,qr->ckr/dot_general | solution.py:87
  203.1 8.5 %fusion.33 = f32[256,32,128]{2,0,1:T(8,128)} fusion(f32[256,32,128]{2,0,1:T(8,128)S(1)} %fusion.18, f32[256,32,128]{2,1,0:T(8,128)S(1)} %get-tuple-element.45), kind=kOutput, calls=%fused_computation.57 | convolution fusion | flops 1611890688 | bytes 12582912 | tf_op jit(solution)/shard_map/ckq,qr->ckr/dot_general | solution.py:87
  211.6 8.7 %fusion.30 = f32[256,32,128]{2,0,1:T(8,128)} fusion(f32[256,32,128]{2,0,1:T(8,128)S(1)} %fusion.20, f32[256,32,128]{2,1,0:T(8,128)S(1)} %get-tuple-element.45), kind=kOutput, calls=%fused_computation.56 | convolution fusion | flops 1611890688 | bytes 12582912 | tf_op jit(solution)/shard_map/ckq,qr->ckr/dot_general | solution.py:84
  220.3 22.4 %multiply_subtract_fusion.1 = (f32[256,32,128]{2,0,1:T(8,128)}, f32[256,32,128]{2,0,1:T(8,128)}, f32[256,32,128]{2,0,1:T(8,128)}, f32[256,32,128]{2,0,1:T(8,128)}) fusion(f32[256,32,128]{2,0,1:T(8,128)} %fusion.36, f32[256,32,128]{2,0,1:T(8,128)} %convolution_add_fusion.1, f32[256,32,128]{2,0,1:T(8,128)} %fusion.39, f32[256,32,128]{2,0,1:T(8,128)} %fusion.33, ...), kind=kOutput, calls=%fused_computation.18 | convolution fusion | flops 1628667904 | bytes 50364416 | tf_op jit(solution)/shard_map/ckq,qr->ckr/dot_general | solution.py:87
  242.7 6.0 %fusion.111 = f32[256,32,128]{2,0,1:T(8,128)S(1)} fusion(f32[256,32,128]{2,0,1:T(8,128)} %get-tuple-element.21), kind=kOutput, calls=%fused_computation.147 | convolution fusion | flops 1610842112 | bytes 8388608 | tf_op jit(solution)/shard_map/ckq,qr->ckr/dot_general | solution.py:96
  248.7 5.8 %fusion.109 = f32[256,32,128]{2,0,1:T(8,128)} fusion(f32[256,32,128]{2,0,1:T(8,128)S(1)} %copy-done.6), kind=kOutput, calls=%fused_computation.145 | convolution fusion | flops 1610842112 | bytes 8388608 | tf_op jit(solution)/shard_map/ckq,qr->ckr/dot_general | solution.py:99
  266.0 4.0 convolution_subtract_fusion.2
  270.0 5.6 %convolution_add_fusion.2 = f32[256,32,128]{2,0,1:T(8,128)} fusion(f32[256,32,128]{2,0,1:T(8,128)S(1)} %fusion.115, f32[256,32,128]{2,0,1:T(8,128)S(1)} %copy-done.4), kind=kOutput, calls=%fused_computation.64 | convolution fusion | flops 1611890688 | bytes 12582912 | tf_op jit(solution)/shard_map/ckq,qr->ckr/dot_general | solution.py:99
  275.6 11.6 %multiply_subtract_fusion = (f32[256,32,128]{2,0,1:T(8,128)}, f32[256,32,128]{2,0,1:T(8,128)}, f32[256,32,128]{2,0,1:T(8,128)}, f32[256,32,128]{2,0,1:T(8,128)}) fusion(f32[256,32,128]{2,0,1:T(8,128)S(1)} %convolution_subtract_fusion, f32[32,128]{1,0:T(8,128)S(1)} %get-tuple-element.46, f32[32,128]{1,0:T(8,128)S(1)} %get-tuple-element.47, ...), kind=kOutput, calls=%fused_computation.17 | convolution fusion | flops 1624473600 | bytes 37781504 | tf_op jit(solution)/shard_map/ckq,qr->ckr/dot_general | solution.py:99
  287.2 7.0 %fusion.6 = f32[256,128,16]{1,2,0:T(8,128)S(1)} fusion(f32[256,32,128]{2,0,1:T(8,128)} %get-tuple-element.42), kind=kOutput, calls=%fused_computation.12 | convolution fusion | flops 201333760 | bytes 6291456 | tf_op jit(solution)/shard_map/kn,ckq->cnq/dot_general | solution.py:104
  294.2 4.9 %fusion.69 = bf16[256,16,128]{2,1,0:T(8,128)(2,1)S(1)} fusion(f32[256,128,16]{1,2,0:T(8,128)S(1)} %fusion.6, f32[256,32,128]{2,0,1:T(8,128)S(1)} %copy-done.9), kind=kOutput, calls=%fused_computation.89 | convolution fusion | flops 202906624 | bytes 7340032 | tf_op jit(solution)/shard_map/kn,ckq->cnq/dot_general | solution.py:104
  302.1 28.8 %select_convert_fusion.1 = bf16[8,273,256]{2,0,1:T(8,128)(2,1)S(1)} fusion(bf16[256,1,128]{0,1,2:T(2,128)(2,1)S(1)} %copy-done.12, bf16[256,1,7,127]{0,2,3,1:T(8,128)(2,1)S(1)} %slice.18, bf16[256,1,8,273]{0,2,3,1:T(8,128)(2,1)S(1)} %copy.115, pred[8,273]{0,1:T(8,128)(4,1)S(1)} %copy-done.13), kind=kOutput, calls=%fused_computation.55 | convolution fusion | flops 149164032 | bytes 2759304 | tf_op jit(solution)/shard_map/conv_general_dilated | solution.py:37
  338.2 5.6 %all-to-all-start.1 = ((bf16[256,8,256]{0,2,1:T(8,128)(2,1)}), bf16[256,8,256]{0,2,1:T(8,128)(2,1)}, u32[]{:S(2)}, u32[]{:S(2)}) async-start(bf16[256,8,256]{0,2,1:T(8,128)(2,1)} %bitcast.19), calls=%async_computation.1 | async-start | bytes 2097152 | tf_op jit(solution)/shard_map/all_to_all | solution.py:152
  343.8 7.0 %fusion.2 = f32[256,128,16]{1,2,0:T(8,128)S(1)} fusion(f32[256,32,128]{2,0,1:T(8,128)} %get-tuple-element.25), kind=kOutput, calls=%fused_computation.7 | convolution fusion | flops 201333760 | bytes 6291456 | tf_op jit(solution)/shard_map/kn,ckq->cnq/dot_general | solution.py:104
  350.8 4.9 %subtract_multiply_fusion = f32[256,128,16]{1,2,0:T(8,128)S(1)} fusion(f32[256,128,16]{1,2,0:T(8,128)S(1)} %fusion.2, f32[256,32,128]{2,0,1:T(8,128)S(1)} %copy-done.10), kind=kOutput, calls=%fused_computation.73 | convolution fusion | flops 202382336 | bytes 8388608 | tf_op jit(solution)/shard_map/kn,ckq->cnq/dot_general | solution.py:104
  361.7 25.4 %fusion.327 = f32[1,256,128]{1,0,2:T(1,128)S(1)} fusion(bf16[1,2184,256]{2,0,1:T(2,128)(2,1)} %reshape.158, bf16[256,1,2048]{0,1,2:T(2,128)(2,1)} %copy.133), kind=kOutput, calls=%fused_computation.345 | convolution fusion | flops 134217728 | bytes 2297856 | tf_op jit(solution)/shard_map/conv_general_dilated | solution.py:37
  388.7 28.6 %fusion.42 = f32[1,256,7]{1,0,2:T(1,128)S(1)} fusion(bf16[1,256,2054]{1,2,0:T(8,128)(2,1)} %slice_bitcast_fusion.1, bf16[256,1,2048]{0,2,1:T(8,128)(2,1)S(1)} %slice_bitcast_fusion.2), kind=kOutput, calls=%fused_computation.66 | convolution fusion | flops 7340032 | bytes 2107392 | tf_op jit(solution)/shard_map/conv_general_dilated | solution.py:37
  (122 shorter events, 89.7 us)
Async XLA Ops:
  0.6 37.9 %copy-start = (bf16[2048,128]{1,0:T(8,128)(2,1)S(1)}, bf16[2048,128]{1,0:T(8,128)(2,1)}, u32[]{:S(2)}) copy-start(bf16[2048,128]{1,0:T(8,128)(2,1)} %param.9) | copy-start | bytes 1572868
  0.6 144.2 %all-to-all-start = ((bf16[8,256,256]{2,1,0:T(8,128)(2,1)}), bf16[8,256,256]{2,1,0:T(8,128)(2,1)}, u32[]{:S(2)}, u32[]{:S(2)}) async-start(bf16[8,256,256]{2,1,0:T(8,128)(2,1)} %bitcast.242), calls=%async_computation | async-start | bytes 2097152 | tf_op jit(solution)/shard_map/all_to_all | solution.py:121
  18.7 23.2 %collective-permute-start = (bf16[256,256]{1,0:T(8,128)(2,1)S(1)}, bf16[256,256]{1,0:T(8,128)(2,1)S(1)}, u32[]{:S(2)}, u32[]{:S(2)}) collective-permute-start(bf16[256,256]{1,0:T(8,128)(2,1)S(1)} %get-tuple-element.40), channel_id=1, source_target_pairs={{0,4},{4,0},{8,12},{12,8},{16,20},{20,16},{24,28},{28,24},{1,5},{5... | collective-permute-start | bytes 393224 | tf_op jit(solution)/shard_map/ppermute | solution.py:28
  20.4 25.5 %collective-permute-start.1 = (bf16[256,256]{1,0:T(8,128)(2,1)S(1)}, bf16[256,256]{1,0:T(8,128)(2,1)S(1)}, u32[]{:S(2)}, u32[]{:S(2)}) collective-permute-start(bf16[256,256]{1,0:T(8,128)(2,1)S(1)} %get-tuple-element.39), channel_id=1, source_target_pairs={{0,8},{4,12},{8,0},{12,4},{16,24},{20,28},{24,16},{28,20},{1,9},{5... | collective-permute-start | bytes 393224 | tf_op jit(solution)/shard_map/ppermute | solution.py:28
  21.9 25.0 %collective-permute-start.2 = (bf16[256,256]{1,0:T(8,128)(2,1)S(1)}, bf16[256,256]{1,0:T(8,128)(2,1)S(1)}, u32[]{:S(2)}, u32[]{:S(2)}) collective-permute-start(bf16[256,256]{1,0:T(8,128)(2,1)S(1)} %get-tuple-element.38), channel_id=1, source_target_pairs={{0,12},{4,8},{8,4},{12,0},{16,28},{20,24},{24,20},{28,16},{1,13},{... | collective-permute-start | bytes 393224 | tf_op jit(solution)/shard_map/ppermute | solution.py:28
  22.2 25.3 %collective-permute-start.3 = (bf16[256,256]{1,0:T(8,128)(2,1)S(1)}, bf16[256,256]{1,0:T(8,128)(2,1)S(1)}, u32[]{:S(2)}, u32[]{:S(2)}) collective-permute-start(bf16[256,256]{1,0:T(8,128)(2,1)S(1)} %get-tuple-element.37), channel_id=1, source_target_pairs={{0,16},{4,20},{8,24},{12,28},{16,0},{20,4},{24,8},{28,12},{1,17},{... | collective-permute-start | bytes 393224 | tf_op jit(solution)/shard_map/ppermute | solution.py:28
  24.8 26.4 %collective-permute-start.4 = (bf16[256,256]{1,0:T(8,128)(2,1)S(1)}, bf16[256,256]{1,0:T(8,128)(2,1)S(1)}, u32[]{:S(2)}, u32[]{:S(2)}) collective-permute-start(bf16[256,256]{1,0:T(8,128)(2,1)S(1)} %get-tuple-element.36), channel_id=1, source_target_pairs={{0,20},{4,16},{8,28},{12,24},{16,4},{20,0},{24,12},{28,8},{1,21},{... | collective-permute-start | bytes 393224 | tf_op jit(solution)/shard_map/ppermute | solution.py:28
  41.9 9.9 %collective-permute-start.5 = (bf16[256,256]{1,0:T(8,128)(2,1)S(1)}, bf16[256,256]{1,0:T(8,128)(2,1)S(1)}, u32[]{:S(2)}, u32[]{:S(2)}) collective-permute-start(bf16[256,256]{1,0:T(8,128)(2,1)S(1)} %get-tuple-element.35), channel_id=1, source_target_pairs={{0,24},{4,28},{8,16},{12,20},{16,8},{20,12},{24,0},{28,4},{1,25},{... | collective-permute-start | bytes 393224 | tf_op jit(solution)/shard_map/ppermute | solution.py:28
  45.9 7.8 %collective-permute-start.6 = (bf16[256,256]{1,0:T(8,128)(2,1)S(1)}, bf16[256,256]{1,0:T(8,128)(2,1)S(1)}, u32[]{:S(2)}, u32[]{:S(2)}) collective-permute-start(bf16[256,256]{1,0:T(8,128)(2,1)S(1)} %get-tuple-element.34), channel_id=1, source_target_pairs={{0,28},{4,24},{8,20},{12,16},{16,12},{20,8},{24,4},{28,0},{1,29},{... | collective-permute-start | bytes 393224 | tf_op jit(solution)/shard_map/ppermute | solution.py:28
  57.0 1.9 copy-start.14
  104.8 14.2 %copy-start.2 = (f32[256,128,32]{1,2,0:T(8,128)S(1)}, f32[256,128,32]{1,2,0:T(8,128)}, u32[]{:S(2)}) copy-start(f32[256,128,32]{1,2,0:T(8,128)} %fusion.166) | copy-start | bytes 12582916
  104.8 14.2 %copy-start.3 = (f32[256,128,32]{1,2,0:T(8,128)S(1)}, f32[256,128,32]{1,2,0:T(8,128)}, u32[]{:S(2)}) copy-start(f32[256,128,32]{1,2,0:T(8,128)} %fusion.158) | copy-start | bytes 12582916
  148.3 3.3 copy-start.8
  242.7 6.0 %copy-start.6 = (f32[256,32,128]{2,0,1:T(8,128)S(1)}, f32[256,32,128]{2,0,1:T(8,128)}, u32[]{:S(2)}) copy-start(f32[256,32,128]{2,0,1:T(8,128)} %get-tuple-element.20) | copy-start | bytes 12582916
  254.6 3.8 copy-start.4
  258.4 3.8 copy-start.5
  270.0 5.6 %copy-start.7 = (f32[256,32,128]{2,0,1:T(8,128)S(1)}, f32[256,32,128]{2,0,1:T(8,128)}, u32[]{:S(2)}) copy-start(f32[256,32,128]{2,0,1:T(8,128)} %get-tuple-element.21) | copy-start | bytes 12582916
  287.2 7.0 %copy-start.9 = (f32[256,32,128]{2,0,1:T(8,128)S(1)}, f32[256,32,128]{2,0,1:T(8,128)}, u32[]{:S(2)}) copy-start(f32[256,32,128]{2,0,1:T(8,128)} %get-tuple-element.43) | copy-start | bytes 12582916
  301.2 0.9 copy-start.12
  301.2 0.9 copy-start.13
  331.0 1.2 copy-start.15
  338.2 79.7 %all-to-all-start.1 = ((bf16[256,8,256]{0,2,1:T(8,128)(2,1)}), bf16[256,8,256]{0,2,1:T(8,128)(2,1)}, u32[]{:S(2)}, u32[]{:S(2)}) async-start(bf16[256,8,256]{0,2,1:T(8,128)(2,1)} %bitcast.19), calls=%async_computation.1 | async-start | bytes 2097152 | tf_op jit(solution)/shard_map/all_to_all | solution.py:152
  343.8 7.0 %copy-start.10 = (f32[256,32,128]{2,0,1:T(8,128)S(1)}, f32[256,32,128]{2,0,1:T(8,128)}, u32[]{:S(2)}) copy-start(f32[256,32,128]{2,0,1:T(8,128)} %get-tuple-element.24) | copy-start | bytes 12582916
  355.7 2.2 copy-start.11
  388.7 31.5 %copy-start.1 = (bf16[2048,128]{1,0:T(8,128)(2,1)S(1)}, bf16[2048,128]{1,0:T(8,128)(2,1)}, u32[]{:S(2)}) copy-start(bf16[2048,128]{1,0:T(8,128)(2,1)} %param.9) | copy-start | bytes 1572868
